TPU v7x, 32 devices: a whole 2x2x4 slice. The times are simulated.
32 devices in a mesh: scene: 2 (over y), az: 8 (over z, x), rg: 2 (over core).
Axes of the slice: x: 2, y: 2, z: 4, core: 2. Of those that a mesh axis runs over, the one named last changes fastest.
Arguments:
- raw_echo: bfloat16 [2, 1024, 4480], P(None, ('scene', 'az'), 'rg'), parts along dimension 1, may hold values from -6 to 6
- chirp: bfloat16 [2, 4096], replicated, may hold values from -0.09375 to 0.09375
- interp_weight: bfloat16 [8, 128], P(None, 'rg'), may hold values from -2 to 2
- band_shift: int32 [128], P('rg'), may hold values from 0 to 248
- doppler_bin: int32 [256], P('scene'), parts along dimension 0, may hold values from -64 to 64
Outputs:
- focused: float32 [256, 2, 512], P(('scene', 'rg', 'az')), parts along dimension 0
There are 2 independent parts, one for each index of `scene`. A program takes and returns all parts, laid end to end along the dimension named above; an argument that names none is the same for every part. Nothing has to cross between parts.
All inputs are finite; a program needn't handle non-finite values.
Results may differ from a plain program's by a relative error of at most 0.0051.
Values may be sent and summed in bfloat16 or wider, within the bound.
A program may use at most 128 MiB of HBM per device.

v0:
```python
import math

import jax
import jax.numpy as jnp
from jax import lax
from jax.sharding import PartitionSpec as P

AZ_TAPS = 2048
AZ_TILE = 128


def partner(value, axis, bit):
    return lax.ppermute(value, axis, [(i, i ^ 1 << bit) for i in range(lax.axis_size(axis))])


def filter_taps(offset, beta, doppler):
    centered = offset - 0.5 * AZ_TAPS
    phase = (
        math.pi * beta * (centered * centered) / AZ_TAPS
        + 2.0 * math.pi / AZ_TAPS * doppler * centered
    )
    amplitude = (0.54 - 0.46 * jnp.cos(2.0 * math.pi / (AZ_TAPS - 1) * offset)) / math.sqrt(
        0.4 * AZ_TAPS
    )
    return (amplitude * jnp.cos(phase), amplitude * jnp.sin(phase))


def shifted_rows(vector, rows):
    taps = vector.shape[0]
    padded = jnp.concatenate([vector, jnp.zeros((rows + 1,), vector.dtype)])
    repeated = jnp.tile(padded, rows)[: rows * (taps + rows)]
    return repeated.reshape(rows, taps + rows)


def range_and_migration(window, kernel, mig_matrix, tile, extent):
    lines = window.shape[1]
    width = kernel.shape[1] // 2
    count = extent // tile
    starts = jnp.arange(count, dtype=jnp.int32) * tile

    def tile_window(start):
        piece = lax.dynamic_slice_in_dim(window, start, width, 2)
        return jnp.concatenate([piece[0], piece[1]], axis=1)

    stacked = jax.vmap(tile_window)(starts).reshape(count * lines, 2 * width)
    tiles_out = lax.dot_general(
        stacked, kernel, (((1,), (1,)), ((), ())), preferred_element_type=jnp.float32
    )
    range_lines = (
        tiles_out.reshape(count, lines, 2, tile).transpose(2, 1, 0, 3).reshape(2 * lines, extent)
    )
    range_lines = range_lines.astype(jnp.bfloat16)
    moved = lax.dot_general(
        mig_matrix, range_lines, (((0,), (1,)), ((), ())), preferred_element_type=jnp.float32
    )
    return moved.astype(jnp.bfloat16).reshape(mig_matrix.shape[1], 2, lines)


def per_device(raw_echo, chirp, interp_weight, band_shift, doppler_bin):
    rg_index = lax.axis_index("rg")
    az_index = lax.axis_index("az")
    half_len = raw_echo.shape[2]
    taps = chirp.shape[1]
    bands = interp_weight.shape[0]
    slab = interp_weight.shape[1]
    extent = 2 * half_len - slab - taps
    tile = min(128, slab)
    margin_len = half_len - slab
    outgoing = lax.dynamic_slice_in_dim(raw_echo, (1 - rg_index) * slab, margin_len, 2)
    incoming = partner(outgoing, "rg", 0)
    window = jnp.where(
        rg_index == 0,
        jnp.concatenate([raw_echo, incoming], axis=2),
        jnp.concatenate([incoming, raw_echo], axis=2),
    )
    rows_re = shifted_rows(chirp[0], tile)
    rows_im = shifted_rows(chirp[1], tile)
    kernel = jnp.concatenate(
        [jnp.concatenate([rows_re, rows_im], axis=1), jnp.concatenate([-rows_im, rows_re], axis=1)],
        axis=0,
    )
    position = lax.broadcasted_iota(jnp.int32, (extent, slab), 0)
    column = lax.broadcasted_iota(jnp.int32, (extent, slab), 1)
    offset = position - column - band_shift[None, :]
    mig_matrix = jnp.zeros((extent, slab), jnp.bfloat16)
    for tap in range(bands):
        mig_matrix = mig_matrix + jnp.where(
            offset == tap, interp_weight[tap][None, :], jnp.zeros((), jnp.bfloat16)
        )
    migrated = range_and_migration(window, kernel, mig_matrix, tile, extent)
    turned = lax.all_to_all(migrated, "az", split_axis=0, concat_axis=2, tiled=True)
    bins_here = turned.shape[0]
    total_lines = turned.shape[2]
    total_bins = slab * lax.axis_size("rg")
    first_bin = rg_index * slab + az_index * bins_here
    doppler = lax.dynamic_slice_in_dim(doppler_bin, first_bin, bins_here).astype(jnp.float32)
    global_bins = (first_bin + jnp.arange(bins_here, dtype=jnp.int32)).astype(jnp.float32)
    beta = 0.5 + 0.5 * global_bins / total_bins
    span = AZ_TAPS // AZ_TILE + 1
    tile_count = total_lines // AZ_TILE
    block_count = (total_lines + AZ_TAPS) // AZ_TILE
    out_index = lax.broadcasted_iota(jnp.int32, (AZ_TILE, AZ_TILE + AZ_TAPS), 0)
    in_index = lax.broadcasted_iota(jnp.int32, (AZ_TILE, AZ_TILE + AZ_TAPS), 1)
    lag = in_index - out_index
    inside = (lag >= 0) & (lag < AZ_TAPS)
    lag_float = lag.astype(jnp.float32)

    def one_bin(args):
        signal, shift, rate = args
        padded = jnp.pad(signal, ((0, 0), (AZ_TAPS // 2, AZ_TAPS // 2)))
        blocks = padded.reshape(2, block_count, AZ_TILE)
        windows = jnp.concatenate(
            [blocks[:, start : start + tile_count] for start in range(span)], axis=2
        )
        left = jnp.concatenate([windows[0], windows[1]], axis=1)
        value_re, value_im = filter_taps(lag_float, rate, shift)
        value_re = jnp.where(inside, value_re, 0.0).astype(jnp.bfloat16)
        value_im = jnp.where(inside, value_im, 0.0).astype(jnp.bfloat16)
        az_kernel = jnp.concatenate(
            [
                jnp.concatenate([value_re, -value_im], axis=1),
                jnp.concatenate([value_im, value_re], axis=1),
            ],
            axis=0,
        )
        result = lax.dot_general(
            left, az_kernel, (((1,), (1,)), ((), ())), preferred_element_type=jnp.float32
        )
        return result.reshape(tile_count, 2, AZ_TILE).transpose(1, 0, 2).reshape(2, total_lines)

    return lax.map(one_bin, (turned, doppler, beta))


def solution(mesh):
    placed = (P(None, ("scene", "az"), "rg"), P(), P(None, "rg"), P("rg"), P("scene"))
    return jax.shard_map(
        per_device,
        mesh=mesh,
        in_specs=placed,
        out_specs=P(("scene", "rg", "az"), None, None),
        check_vma=False,
    )
```

profile of v0, /device:TPU:0, one launch (start us, length us, event | category | flops | bytes accessed | tf_op | source)
XLA Modules:
  0.0 197.8 jit_solution(17138501759264613210)
XLA Ops:
  0.0 1.3 constant_dynamic-slice_fusion.1
  1.3 0.5 collective-permute-start
  2.0 0.6 tile.21
  2.6 0.4 reshape.61
  3.2 0.6 tile.9
  4.4 1.8 fusion.41
  6.6 12.9 %while.15 = (s32[]{:T(128)}, bf16[2,64,4416]{2,1,0:T(8,128)(2,1)S(1)}, s32[5,3]{0,1:T(4,128)S(1)}, bf16[5,2,64,4160]{3,2,0,1:T(8,128)(2,1)}, s32[]{:T(128)}) while((s32[]{:T(128)}, bf16[2,64,4416]{2,1,0:T(8,128)(2,1)S(1)}, s32[5,3]{0,1:T(4,128)S(1)}, bf16[5,2,64,4160]{3,2,0,1:T(8,128)(2,1)}, s32[]{:T(128)}) %tuple.58), condition=%wide.while_cond, body=%wide.while_body.sunk | while | flops 2 | bytes 2147425 | solution.py:42
  6.7 0.5 slice.294
  7.2 2.0 bitcast_dynamic-update-slice_fusion.4
  9.3 0.5 slice.294
  9.8 2.0 bitcast_dynamic-update-slice_fusion.4
  11.9 0.5 slice.294
  12.4 2.0 %bitcast_dynamic-update-slice_fusion.4 = bf16[5,2,64,4160]{3,2,0,1:T(8,128)(2,1)} fusion(bf16[5,2,64,4160]{3,2,0,1:T(8,128)(2,1)} %get-tuple-element.258, s32[]{:T(128)} %get-tuple-element.255, bf16[2,64,4416]{2,1,0:T(8,128)(2,1)S(1)} %get-tuple-element.261, s32[]{:T(128)} %bitcast.69), kind=kLoop, calls=%fused_computation.2.clone.1 | loop fusion | bytes 2147328 | tf_op jit(solution)/shard_map/vmap()/gather
  14.5 0.5 slice.294
  15.0 2.0 bitcast_dynamic-update-slice_fusion.4
  17.1 0.5 slice.294
  17.6 1.9 bitcast_dynamic-update-slice_fusion.4
  19.5 3.1 %slice_bitcast_fusion.3 = (bf16[5,64,4160]{2,1,0:T(8,128)(2,1)S(1)}, bf16[5,64,4160]{2,1,0:T(8,128)(2,1)S(1)}) fusion(bf16[5,2,64,4160]{3,2,0,1:T(8,128)(2,1)} %get-tuple-element.115), kind=kLoop, calls=%fused_computation.65 | loop fusion | bytes 10649600 | tf_op jit(solution)/shard_map/vmap()/concatenate | solution.py:43
  22.8 1.6 fusion.43
  25.1 0.7 reshape.94
  25.8 6.8 %all-to-all-start = ((bf16[8,2,512]{2,1,0:T(2,128)(2,1)}), bf16[8,2,512]{2,1,0:T(2,128)(2,1)S(1)}, u32[]{:S(2)}, u32[]{:S(2)}) async-start(bf16[8,2,512]{2,1,0:T(2,128)(2,1)} %reshape.94), calls=%async_computation | async-start | bytes 32768 | tf_op jit(solution)/shard_map/all_to_all | solution.py:91
  32.7 6.5 %all-to-all-done = bf16[8,2,512]{2,1,0:T(2,128)(2,1)S(1)} async-done(((bf16[8,2,512]{2,1,0:T(2,128)(2,1)}), bf16[8,2,512]{2,1,0:T(2,128)(2,1)S(1)}, u32[]{:S(2)}, u32[]{:S(2)}) %all-to-all-start) | async-done | bytes 16416 | tf_op jit(solution)/shard_map/all_to_all | solution.py:91
  39.4 157.7 %while.16 = (s32[]{:T(128)}, f32[8,2,512]{2,1,0:T(2,128)S(1)}, bf16[8,2,512]{2,1,0:T(2,128)(2,1)S(1)}, f32[8]{0:T(128)S(1)}, f32[8]{0:T(128)S(1)}, /*index=5*/s32[]{:T(128)}, f32[1]{0:T(128)}, f32[1]{0:T(128)}, bf16[]{:T(256)}) while((s32[]{:T(128)}, f32[8,2,512]{2,1,0:T(2,128)S(1)}, bf16[8,2,512]{2,1,0:T(2,128)(2,1)S(1)}, ...), condition=%wide.region_1.2_spmd.clone.clone, body=%wide.region_0.1_spmd.clone.clone.sunk | while | flops 29593604 | bytes 3573927 | solution.py:131
  39.7 0.6 dynamic_slice.41
  41.0 0.7 dynamic_slice.42
  42.2 8.2 %fusion.112 = (bf16[128,2176]{1,0:T(8,128)(2,1)S(1)}, bf16[128,2176]{1,0:T(8,128)(2,1)S(1)}) fusion(f32[]{:T(128)} %bitcast.73, f32[]{:T(128)} %bitcast.74), kind=kLoop, calls=%fused_computation.30.clone.1 | loop fusion | flops 5849088 | bytes 1114120 | tf_op jit(solution)/shard_map/while/body/eval_jaxpr/convert_element_type | solution.py:117
  50.5 7.9 %fusion.113 = bf16[128,2176]{1,0:T(8,128)(2,1)S(1)} fusion(f32[]{:T(128)} %bitcast.73, f32[]{:T(128)} %bitcast.74), kind=kLoop, calls=%fused_computation.34.clone.1 | loop fusion | flops 5849088 | bytes 557064 | tf_op jit(solution)/shard_map/while/body/eval_jaxpr/neg | solution.py:121
  58.4 0.7 fusion.114
  59.4 0.6 dynamic_slice.41
  60.7 0.7 dynamic_slice.42
  62.0 8.2 %fusion.112 = (bf16[128,2176]{1,0:T(8,128)(2,1)S(1)}, bf16[128,2176]{1,0:T(8,128)(2,1)S(1)}) fusion(f32[]{:T(128)} %bitcast.73, f32[]{:T(128)} %bitcast.74), kind=kLoop, calls=%fused_computation.30.clone.1 | loop fusion | flops 5849088 | bytes 1114120 | tf_op jit(solution)/shard_map/while/body/eval_jaxpr/convert_element_type | solution.py:117
  70.2 7.9 %fusion.113 = bf16[128,2176]{1,0:T(8,128)(2,1)S(1)} fusion(f32[]{:T(128)} %bitcast.73, f32[]{:T(128)} %bitcast.74), kind=kLoop, calls=%fused_computation.34.clone.1 | loop fusion | flops 5849088 | bytes 557064 | tf_op jit(solution)/shard_map/while/body/eval_jaxpr/neg | solution.py:121
  78.1 0.7 fusion.114
  79.2 0.6 dynamic_slice.41
  80.4 0.7 dynamic_slice.42
  81.7 8.2 %fusion.112 = (bf16[128,2176]{1,0:T(8,128)(2,1)S(1)}, bf16[128,2176]{1,0:T(8,128)(2,1)S(1)}) fusion(f32[]{:T(128)} %bitcast.73, f32[]{:T(128)} %bitcast.74), kind=kLoop, calls=%fused_computation.30.clone.1 | loop fusion | flops 5849088 | bytes 1114120 | tf_op jit(solution)/shard_map/while/body/eval_jaxpr/convert_element_type | solution.py:117
  89.9 7.9 %fusion.113 = bf16[128,2176]{1,0:T(8,128)(2,1)S(1)} fusion(f32[]{:T(128)} %bitcast.73, f32[]{:T(128)} %bitcast.74), kind=kLoop, calls=%fused_computation.34.clone.1 | loop fusion | flops 5849088 | bytes 557064 | tf_op jit(solution)/shard_map/while/body/eval_jaxpr/neg | solution.py:121
  97.8 0.7 fusion.114
  98.9 0.6 dynamic_slice.41
  100.1 0.7 dynamic_slice.42
  101.4 8.2 %fusion.112 = (bf16[128,2176]{1,0:T(8,128)(2,1)S(1)}, bf16[128,2176]{1,0:T(8,128)(2,1)S(1)}) fusion(f32[]{:T(128)} %bitcast.73, f32[]{:T(128)} %bitcast.74), kind=kLoop, calls=%fused_computation.30.clone.1 | loop fusion | flops 5849088 | bytes 1114120 | tf_op jit(solution)/shard_map/while/body/eval_jaxpr/convert_element_type | solution.py:117
  109.6 7.9 %fusion.113 = bf16[128,2176]{1,0:T(8,128)(2,1)S(1)} fusion(f32[]{:T(128)} %bitcast.73, f32[]{:T(128)} %bitcast.74), kind=kLoop, calls=%fused_computation.34.clone.1 | loop fusion | flops 5849088 | bytes 557064 | tf_op jit(solution)/shard_map/while/body/eval_jaxpr/neg | solution.py:121
  117.5 0.7 fusion.114
  118.6 0.6 dynamic_slice.41
  119.8 0.7 dynamic_slice.42
  121.1 8.2 %fusion.112 = (bf16[128,2176]{1,0:T(8,128)(2,1)S(1)}, bf16[128,2176]{1,0:T(8,128)(2,1)S(1)}) fusion(f32[]{:T(128)} %bitcast.73, f32[]{:T(128)} %bitcast.74), kind=kLoop, calls=%fused_computation.30.clone.1 | loop fusion | flops 5849088 | bytes 1114120 | tf_op jit(solution)/shard_map/while/body/eval_jaxpr/convert_element_type | solution.py:117
  129.3 7.9 %fusion.113 = bf16[128,2176]{1,0:T(8,128)(2,1)S(1)} fusion(f32[]{:T(128)} %bitcast.73, f32[]{:T(128)} %bitcast.74), kind=kLoop, calls=%fused_computation.34.clone.1 | loop fusion | flops 5849088 | bytes 557064 | tf_op jit(solution)/shard_map/while/body/eval_jaxpr/neg | solution.py:121
  137.2 0.7 fusion.114
  138.3 0.6 dynamic_slice.41
  139.5 0.7 dynamic_slice.42
  140.8 8.2 %fusion.112 = (bf16[128,2176]{1,0:T(8,128)(2,1)S(1)}, bf16[128,2176]{1,0:T(8,128)(2,1)S(1)}) fusion(f32[]{:T(128)} %bitcast.73, f32[]{:T(128)} %bitcast.74), kind=kLoop, calls=%fused_computation.30.clone.1 | loop fusion | flops 5849088 | bytes 1114120 | tf_op jit(solution)/shard_map/while/body/eval_jaxpr/convert_element_type | solution.py:117
  149.0 7.9 %fusion.113 = bf16[128,2176]{1,0:T(8,128)(2,1)S(1)} fusion(f32[]{:T(128)} %bitcast.73, f32[]{:T(128)} %bitcast.74), kind=kLoop, calls=%fused_computation.34.clone.1 | loop fusion | flops 5849088 | bytes 557064 | tf_op jit(solution)/shard_map/while/body/eval_jaxpr/neg | solution.py:121
  157.0 0.7 fusion.114
  158.0 0.6 dynamic_slice.41
  159.3 0.7 dynamic_slice.42
  160.5 8.2 %fusion.112 = (bf16[128,2176]{1,0:T(8,128)(2,1)S(1)}, bf16[128,2176]{1,0:T(8,128)(2,1)S(1)}) fusion(f32[]{:T(128)} %bitcast.73, f32[]{:T(128)} %bitcast.74), kind=kLoop, calls=%fused_computation.30.clone.1 | loop fusion | flops 5849088 | bytes 1114120 | tf_op jit(solution)/shard_map/while/body/eval_jaxpr/convert_element_type | solution.py:117
  168.8 7.9 %fusion.113 = bf16[128,2176]{1,0:T(8,128)(2,1)S(1)} fusion(f32[]{:T(128)} %bitcast.73, f32[]{:T(128)} %bitcast.74), kind=kLoop, calls=%fused_computation.34.clone.1 | loop fusion | flops 5849088 | bytes 557064 | tf_op jit(solution)/shard_map/while/body/eval_jaxpr/neg | solution.py:121
  176.7 0.7 fusion.114
  177.7 0.6 dynamic_slice.41
  179.0 0.7 dynamic_slice.42
  180.3 8.2 %fusion.112 = (bf16[128,2176]{1,0:T(8,128)(2,1)S(1)}, bf16[128,2176]{1,0:T(8,128)(2,1)S(1)}) fusion(f32[]{:T(128)} %bitcast.73, f32[]{:T(128)} %bitcast.74), kind=kLoop, calls=%fused_computation.30.clone.1 | loop fusion | flops 5849088 | bytes 1114120 | tf_op jit(solution)/shard_map/while/body/eval_jaxpr/convert_element_type | solution.py:117
  188.5 7.9 %fusion.113 = bf16[128,2176]{1,0:T(8,128)(2,1)S(1)} fusion(f32[]{:T(128)} %bitcast.73, f32[]{:T(128)} %bitcast.74), kind=kLoop, calls=%fused_computation.34.clone.1 | loop fusion | flops 5849088 | bytes 557064 | tf_op jit(solution)/shard_map/while/body/eval_jaxpr/neg | solution.py:121
  196.4 0.7 fusion.114
  197.1 0.6 copy-done.4
  (227 shorter events, 5.3 us)
Async XLA Ops:
  0.0 1.8 copy-start.2
  1.3 4.9 %collective-permute-start = (bf16[2,64,2176]{2,1,0:T(8,128)(2,1)S(1)}, bf16[2,64,2176]{2,1,0:T(8,128)(2,1)S(1)}, u32[]{:S(2)}, u32[]{:S(2)}) collective-permute-start(bf16[2,64,2176]{2,1,0:T(8,128)(2,1)S(1)} %constant_dynamic-slice_fusion.1), channel_id=1, source_target_pairs={{0,1},{1,0},{2,3},{3,2},{4,5},{5,4},{6,7},{7,6},{8,9},{9,8},{10,11... | collective-permute-start | bytes 1671176 | tf_op jit(solution)/shard_map/ppermute | solution.py:13
  4.3 1.8 copy-start.3
  4.3 1.8 copy-start
  19.5 3.2 %copy-start.1 = (bf16[128,8320]{1,0:T(8,128)(2,1)S(1)}, bf16[128,8320]{1,0:T(8,128)(2,1)}, u32[]{:S(2)}) copy-start(bf16[128,8320]{1,0:T(8,128)(2,1)} %fusion.41) | copy-start | bytes 6389764
  22.8 1.9 copy-start.5
  24.4 8.2 %copy-start.6 = (s32[128]{0:T(128)S(1)}, s32[128]{0:T(128)}, u32[]{:S(2)}) copy-start(s32[128]{0:T(128)} %param.11) | copy-start | bytes 1540
  25.8 13.4 %all-to-all-start = ((bf16[8,2,512]{2,1,0:T(2,128)(2,1)}), bf16[8,2,512]{2,1,0:T(2,128)(2,1)S(1)}, u32[]{:S(2)}, u32[]{:S(2)}) async-start(bf16[8,2,512]{2,1,0:T(2,128)(2,1)} %reshape.94), calls=%async_computation | async-start | bytes 32768 | tf_op jit(solution)/shard_map/all_to_all | solution.py:91
  197.1 0.6 copy-start.4
where the time goes:
time: 198 us
  other arithmetic  131 us (66%)
  local copies, waits for them, and re-layouts  34.2 us (17%)
  loops' own time  11.1 us (6%)
  starting transfers between devices  7.34 us (4%)
  matrix products  7.16 us (4%)
  waiting for transfers between devices  6.49 us (3%)
    convert_element_type x8, other arithmetic, one_bin(): value_re = jnp.where(inside, value_re, 0.0).astype(jnp.bfloat16)  65.7 us
    neg x8, other arithmetic, one_bin(): -value_im  63.2 us
    gather x15, local copies, waits for them, and re-layouts  12.9 us
    another operation x1, loops' own time, per_device(): return lax.map(one_bin, (turned, doppler, beta))  11 us
    dynamic_slice x16, local copies, waits for them, and re-layouts, per_device(): return lax.map(one_bin, (turned, doppler, beta))  9.93 us
    all_to_all x1, starting transfers between devices, per_device(): lax.all_to_all(migrated, 'az', split_axis=0, concat_axis=2, tiled=True)  6.82 us
    all_to_all x1, waiting for transfers between devices, per_device(): lax.all_to_all(migrated, 'az', split_axis=0, concat_axis=2, tiled=True)  6.49 us
    dot_general x8, matrix products, one_bin(): lax.dot_general(left, az_kernel, (((1,), (1,)), ((), ())), preferred_elem...  5.24 us
  transfers between devices with their start and end apart: 2, of which 1 were waited for; matrix products, arithmetic and copies ran while one was open for 2% of the time, Pallas kernels for 0%

commit v1 on v0

--- a/solution.py
+++ b/solution.py
@@ -1,12 +1,17 @@
+import functools
 import math
 
 import jax
 import jax.numpy as jnp
 from jax import lax
+from jax.experimental import pallas as pl
+from jax.experimental.pallas import tpu as pltpu
 from jax.sharding import PartitionSpec as P
 
 AZ_TAPS = 2048
 AZ_TILE = 128
+TILE = 128
+MESH = pl.DeviceIdType.MESH
 
 
 def partner(value, axis, bit):
@@ -131,10 +136,197 @@
     return lax.map(one_bin, (turned, doppler, beta))
 
 
+def toeplitz_rows(row, rows):
+    return pltpu.roll(jnp.broadcast_to(row, (rows, row.shape[1])), 0, 1, stride=1, stride_axis=0)
+
+
+def column(row, first, rows):
+    width = row.shape[1]
+    lane = lax.broadcasted_iota(jnp.int32, (rows, width), 1)
+    sub = lax.broadcasted_iota(jnp.int32, (rows, width), 0)
+    picked = jnp.where(lane == sub + first, jnp.broadcast_to(row, (rows, width)), 0.0)
+    return jnp.sum(picked, axis=1, keepdims=True)
+
+
+def dot_nt(left, right):
+    return lax.dot_general(
+        left, right, (((1,), (1,)), ((), ())), preferred_element_type=jnp.float32
+    )
+
+
+def fused_kernel(
+    azs, raw, chirp, weight, shift, doppler, out,
+    halves, full, chirp_rows, az_rows, moved, slots, spread,
+    local_sem, pair_send, pair_recv, turn_send, turn_recv,
+):
+    az = lax.axis_index("az")
+    rg = lax.axis_index("rg")
+    lines = raw.shape[1]
+    slab = weight.shape[1]
+    bins = out.shape[0]
+    tiles_az = out.shape[2]
+    taps = chirp.shape[1]
+    width = taps + TILE
+    extent = full.shape[1] - taps
+
+    barrier = pltpu.get_barrier_semaphore()
+    pl.semaphore_signal(barrier, inc=1, device_id={"rg": 1 - rg}, device_id_type=MESH)
+    for step in range(1, azs):
+        pl.semaphore_signal(
+            barrier, inc=1, device_id={"az": lax.rem(az + step, azs)}, device_id_type=MESH
+        )
+    own = pltpu.make_async_copy(raw, halves.at[rg], local_sem)
+    own.start()
+    pl.semaphore_wait(barrier, azs)
+    pair = pltpu.make_async_remote_copy(
+        src_ref=raw, dst_ref=halves.at[rg], send_sem=pair_send, recv_sem=pair_recv,
+        device_id={"rg": 1 - rg}, device_id_type=MESH,
+    )
+    pair.start()
+
+    for part in range(2):
+        padded = jnp.concatenate(
+            [chirp[part : part + 1, :].astype(jnp.float32), jnp.zeros((1, TILE), jnp.float32)],
+            axis=1,
+        )
+        chirp_rows[part * TILE : (part + 1) * TILE, :] = toeplitz_rows(padded, TILE).astype(
+            jnp.bfloat16
+        )
+
+    span = (2 * tiles_az - 1) * TILE
+    wheel = span + TILE
+    first_bin = rg * slab + az * bins
+    place = lax.broadcasted_iota(jnp.int32, (bins, wheel), 1)
+    lag = place + AZ_TAPS // 2 - (tiles_az - 1) * TILE - jnp.where(place >= span, wheel, 0)
+    bin_index = first_bin + lax.broadcasted_iota(jnp.int32, (bins, wheel), 0)
+    beta = 0.5 + 0.5 * bin_index.astype(jnp.float32) / (2 * slab)
+    rate = column(doppler[...].astype(jnp.float32), first_bin, bins)
+    value_re, value_im = filter_taps(lag.astype(jnp.float32), beta, rate)
+    for part, value in enumerate((value_re, value_im)):
+        value = value.astype(jnp.bfloat16).astype(jnp.float32)
+        for b in range(bins):
+            rows = toeplitz_rows(value[b : b + 1, :], TILE)
+            az_rows[b, part * TILE : (part + 1) * TILE, :] = rows[:, :span].astype(jnp.bfloat16)
+
+    position = lax.broadcasted_iota(jnp.int32, (slab, extent), 1)
+    bin_at = lax.broadcasted_iota(jnp.int32, (slab, extent), 0) + rg * slab
+    start = column(shift[...].astype(jnp.float32), 0, slab).astype(jnp.int32)
+    offset = position - bin_at - start
+    mig = jnp.zeros((slab, extent), jnp.float32)
+    for tap in range(weight.shape[0]):
+        tap_weight = column(weight[tap : tap + 1, :].astype(jnp.float32), 0, slab)
+        mig = jnp.where(offset == tap, tap_weight, mig)
+    mig = mig.astype(jnp.bfloat16)
+
+    own.wait()
+    pair.wait()
+    half_len = raw.shape[2]
+    full[...] = jnp.concatenate(
+        [halves[0].reshape(2 * lines, half_len), halves[1].reshape(2 * lines, half_len)], axis=1
+    )
+    kernel = chirp_rows[...]
+    pieces = []
+    for t in range(extent // TILE):
+        product = dot_nt(full[:, t * TILE : t * TILE + width], kernel)
+        real = product[:lines, :TILE] + product[lines:, TILE:]
+        imag = product[lines:, :TILE] - product[:lines, TILE:]
+        pieces.append(jnp.concatenate([real, imag], axis=0).astype(jnp.bfloat16))
+    range_lines = jnp.concatenate(pieces, axis=1)
+    moved[...] = dot_nt(mig, range_lines).astype(jnp.bfloat16).astype(jnp.float32)
+
+    def block(index):
+        return moved.at[pl.ds(pl.multiple_of(index * bins, bins), bins), :]
+
+    copies = []
+    for step in range(1, azs):
+        peer = lax.rem(az + step, azs)
+        copy = pltpu.make_async_remote_copy(
+            src_ref=block(peer), dst_ref=slots.at[az], send_sem=turn_send.at[step],
+            recv_sem=turn_recv.at[az], device_id={"az": peer}, device_id_type=MESH,
+        )
+        copy.start()
+        copies.append(copy)
+    slots[az] = block(az)[...]
+    for step in range(1, azs):
+        peer = lax.rem(az + step, azs)
+        pltpu.make_async_remote_copy(
+            src_ref=block(peer), dst_ref=slots.at[peer], send_sem=turn_send.at[step],
+            recv_sem=turn_recv.at[peer], device_id={"az": peer}, device_id_type=MESH,
+        ).wait_recv()
+
+    apron = jnp.zeros((bins, (tiles_az - 1) * TILE), jnp.float32)
+    for part in range(2):
+        signal = jnp.concatenate(
+            [slots[i][:, part * lines : (part + 1) * lines] for i in range(azs)], axis=1
+        )
+        signal = jnp.concatenate([apron, signal, apron], axis=1)
+        for t in range(tiles_az):
+            spread[part * tiles_az + t] = signal[:, t * TILE : t * TILE + span]
+    for b in range(bins):
+        product = dot_nt(spread[:, b, :].astype(jnp.bfloat16), az_rows[b])
+        out[b, 0] = product[:tiles_az, :TILE] - product[tiles_az:, TILE:]
+        out[b, 1] = product[tiles_az:, :TILE] + product[:tiles_az, TILE:]
+    for copy in copies:
+        copy.wait_send()
+
+
+def fused(raw_echo, chirp, interp_weight, band_shift, doppler_bin):
+    azs = lax.axis_size("az")
+    lines, half_len = raw_echo.shape[1:]
+    taps = chirp.shape[1]
+    slab = interp_weight.shape[1]
+    bins = slab // azs
+    tiles_az = azs * lines // TILE
+    span = (2 * tiles_az - 1) * TILE
+    vmem = pl.BlockSpec(memory_space=pltpu.VMEM)
+    result = pl.pallas_call(
+        functools.partial(fused_kernel, azs),
+        out_shape=jax.ShapeDtypeStruct((bins, 2, tiles_az, TILE), jnp.float32),
+        in_specs=[pl.BlockSpec(memory_space=pl.ANY), vmem, vmem, vmem, vmem],
+        out_specs=vmem,
+        scratch_shapes=[
+            pltpu.VMEM((2, 2, lines, half_len), jnp.bfloat16),
+            pltpu.VMEM((2 * lines, 2 * half_len), jnp.bfloat16),
+            pltpu.VMEM((2 * TILE, taps + TILE), jnp.bfloat16),
+            pltpu.VMEM((bins, 2 * TILE, span), jnp.bfloat16),
+            pltpu.VMEM((slab, 2 * lines), jnp.float32),
+            pltpu.VMEM((azs, bins, 2 * lines), jnp.float32),
+            pltpu.VMEM((2 * tiles_az, bins, span), jnp.float32),
+            pltpu.SemaphoreType.DMA,
+            pltpu.SemaphoreType.DMA,
+            pltpu.SemaphoreType.DMA,
+            pltpu.SemaphoreType.DMA((azs,)),
+            pltpu.SemaphoreType.DMA((azs,)),
+        ],
+        compiler_params=pltpu.CompilerParams(
+            collective_id=0, has_side_effects=True, vmem_limit_bytes=48 * 1024 * 1024
+        ),
+    )(raw_echo, chirp, interp_weight, band_shift.reshape(1, -1), doppler_bin.reshape(1, -1))
+    return result.reshape(bins, 2, tiles_az * TILE)
+
+
+def local(raw_echo, chirp, interp_weight, band_shift, doppler_bin):
+    azs = lax.axis_size("az")
+    lines, half_len = raw_echo.shape[1:]
+    total_lines = azs * lines
+    extent = 2 * half_len - chirp.shape[1]
+    small = (
+        lax.axis_size("rg") == 2
+        and interp_weight.shape[1] == 8 * azs
+        and 2 * lines == TILE
+        and total_lines % TILE == 0
+        and total_lines <= AZ_TAPS // 4
+        and extent % TILE == 0
+        and extent <= 512
+    )
+    run = fused if small else per_device
+    return run(raw_echo, chirp, interp_weight, band_shift, doppler_bin)
+
+
 def solution(mesh):
     placed = (P(None, ("scene", "az"), "rg"), P(), P(None, "rg"), P("rg"), P("scene"))
     return jax.shard_map(
-        per_device,
+        local,
         mesh=mesh,
         in_specs=placed,
         out_specs=P(("scene", "rg", "az"), None, None),

time: 198 us -> 18.3 us (0.09)
  other arithmetic: 131 us -> 0 us
  local copies, waits for them, and re-layouts: 34.2 us -> 3.11 us
  Pallas kernels: 0 us -> 14.9 us
  loops' own time: 11.1 us -> 0 us
  starting transfers between devices: 7.34 us -> 0 us
  matrix products: 7.16 us -> 0 us
  waiting for transfers between devices: 6.49 us -> 0 us
    convert_element_type x9 -> x0, other arithmetic: 65.8 us -> none  [the longest x8 65.7 us: one_bin(): value_re = jnp.where(inside, value_re, 0.0).astype(jnp.bfloat16)]
    neg x9 -> x0, other arithmetic: 63.2 us -> none  [the longest x8 63.2 us: one_bin(): -value_im]
    pallas_call x0 -> x1, Pallas kernels: none -> 14.9 us  [fused(): pl.pallas_call(functools.partial(fused_kernel, azs), out_shape=jax.ShapeD...]
    gather x15 -> x0, local copies, waits for them, and re-layouts: 12.9 us -> none
    dynamic_slice x17 -> x0, local copies, waits for them, and re-layouts: 11.2 us -> none  [the longest x16 9.93 us: per_device(): return lax.map(one_bin, (turned, doppler, beta))]
    another operation x2 -> x0, loops' own time: 11.1 us -> none  [the longest x1 11 us: per_device(): return lax.map(one_bin, (turned, doppler, beta))]
    dot_general x10 -> x0, matrix products: 7.16 us -> none  [the longest x8 5.24 us: one_bin(): lax.dot_general(left, az_kernel, (((1,), (1,)), ((), ())), preferred_elem...]
    all_to_all x1 -> x0, starting transfers between devices: 6.82 us -> none  [per_device(): lax.all_to_all(migrated, 'az', split_axis=0, concat_axis=2, tiled=True)]
  transfers between devices with their start and end apart: 2 -> 0, of which waited for: 1 -> 0; matrix products, arithmetic and copies ran while one was open for 2% -> 0% of each run, Pallas kernels for 0% -> 0%
where the time goes in v1:
time: 18.3 us; the launch traced here: 18 us
  Pallas kernels  14.9 us (81%)
  local copies, waits for them, and re-layouts  3.11 us (17%)
    pallas_call x1, Pallas kernels, fused(): pl.pallas_call(functools.partial(fused_kernel, azs), out_shape=jax.ShapeD...  14.9 us
    unnamed x10, local copies, waits for them, and re-layouts  2.47 us
    reshape x1, local copies, waits for them, and re-layouts, fused(): return result.reshape(bins, 2, tiles_az * TILE)  0.64 us

profile of v1, /device:TPU:0, one launch (start us, length us, event | category | flops | bytes accessed | tf_op | source)
XLA Modules:
  0.0 18.0 jit_solution(18068448548013894720)
XLA Ops:
  0.0 0.0 copy-start.2
  0.0 0.0 copy-start.3
  0.0 0.0 copy-start.4
  0.0 0.7 %copy-done.2 = bf16[8,64]{1,0:T(8,128)(2,1)S(1)} copy-done((bf16[8,64]{1,0:T(8,128)(2,1)S(1)}, bf16[8,64]{1,0:T(8,128)(2,1)}, u32[]{:S(2)}) %copy-start.2) | copy-done | bytes 1048
  0.7 0.0 copy-done.3
  0.7 0.0 copy-done.4
  0.7 0.0 copy-start
  0.7 1.1 %copy-done = bf16[2,64,2240]{2,1,0:T(8,128)(2,1)S(1)} copy-done((bf16[2,64,2240]{2,1,0:T(8,128)(2,1)S(1)}, bf16[2,64,2240]{2,1,0:T(8,128)(2,1)}, u32[]{:S(2)}) %copy-start) | copy-done | bytes 573464
  1.8 0.0 copy-start.1
  1.8 0.7 %copy-done.1 = bf16[2,4096]{1,0:T(2,128)(2,1)S(1)} copy-done((bf16[2,4096]{1,0:T(2,128)(2,1)S(1)}, bf16[2,4096]{1,0:T(2,128)(2,1)}, u32[]{:S(2)}) %copy-start.1) | copy-done | bytes 16408
  2.5 14.9 %shard_map.55 = f32[8,2,4,128]{3,2,1,0:T(4,128)S(1)} custom-call(bf16[2,64,2240]{2,1,0:T(8,128)(2,1)S(1)} %copy-done, bf16[2,4096]{1,0:T(2,128)(2,1)S(1)} %copy-done.1, bf16[8,64]{1,0:T(8,128)(2,1)S(1)} %copy-done.2, s32[1,64]{1,0:T(1,128)S(1)} %bitcast.2, s32[1,128]{1,0:T(1,128)S(1)} %bitcast.3), custom_call_target="tpu_custom_call" | custom-call | tf_op jit(solution)/shard_map/pallas_call | solution.py:282
  17.4 0.6 %reshape.11 = f32[8,2,512]{2,1,0:T(2,128)} reshape(f32[8,2,4,128]{3,2,1,0:T(4,128)S(1)} %shard_map.55) | data formatting | bytes 65536 | tf_op jit(solution)/shard_map/reshape | solution.py:305
Async XLA Ops:
  0.0 0.7 %copy-start.2 = (bf16[8,64]{1,0:T(8,128)(2,1)S(1)}, bf16[8,64]{1,0:T(8,128)(2,1)}, u32[]{:S(2)}) copy-start(bf16[8,64]{1,0:T(8,128)(2,1)} %weight.1) | copy-start | bytes 3076
  0.0 0.7 %copy-start.3 = (s32[64]{0:T(128)S(1)}, s32[64]{0:T(128)}, u32[]{:S(2)}) copy-start(s32[64]{0:T(128)} %param.8) | copy-start | bytes 772
  0.0 0.7 %copy-start.4 = (s32[128]{0:T(128)S(1)}, s32[128]{0:T(128)}, u32[]{:S(2)}) copy-start(s32[128]{0:T(128)} %param.9) | copy-start | bytes 1540
  0.7 1.1 %copy-start = (bf16[2,64,2240]{2,1,0:T(8,128)(2,1)S(1)}, bf16[2,64,2240]{2,1,0:T(8,128)(2,1)}, u32[]{:S(2)}) copy-start(bf16[2,64,2240]{2,1,0:T(8,128)(2,1)} %raw.1) | copy-start | bytes 1720324
  1.8 0.7 %copy-start.1 = (bf16[2,4096]{1,0:T(2,128)(2,1)S(1)}, bf16[2,4096]{1,0:T(2,128)(2,1)}, u32[]{:S(2)}) copy-start(bf16[2,4096]{1,0:T(2,128)(2,1)} %chirp.1) | copy-start | bytes 49156

commit v2 on v1

--- a/solution.py
+++ b/solution.py
@@ -155,14 +155,14 @@
 
 
 def fused_kernel(
-    azs, raw, chirp, weight, shift, doppler, out,
-    halves, full, chirp_rows, az_rows, moved, slots, spread,
+    azs, raw, chirp_in, weight_in, shift_in, doppler_in, out,
+    chirp, weight, shift, doppler, small_sem, halves, full, chirp_rows, az_rows, moved, slots, spread, sums,
     local_sem, pair_send, pair_recv, turn_send, turn_recv,
 ):
     az = lax.axis_index("az")
     rg = lax.axis_index("rg")
     lines = raw.shape[1]
-    slab = weight.shape[1]
+    slab = weight_in.shape[1]
     bins = out.shape[0]
     tiles_az = out.shape[2]
     taps = chirp.shape[1]
@@ -175,6 +175,14 @@
         pl.semaphore_signal(
             barrier, inc=1, device_id={"az": lax.rem(az + step, azs)}, device_id_type=MESH
         )
+    loads = [
+        pltpu.make_async_copy(source, target, small_sem.at[i])
+        for i, (source, target) in enumerate(
+            ((chirp_in, chirp), (doppler_in, doppler), (shift_in, shift), (weight_in, weight))
+        )
+    ]
+    for load in loads:
+        load.start()
     own = pltpu.make_async_copy(raw, halves.at[rg], local_sem)
     own.start()
     pl.semaphore_wait(barrier, azs)
@@ -183,6 +191,9 @@
         device_id={"rg": 1 - rg}, device_id_type=MESH,
     )
     pair.start()
+
+    for load in loads:
+        load.wait()
 
     for part in range(2):
         padded = jnp.concatenate(
@@ -218,16 +229,48 @@
         mig = jnp.where(offset == tap, tap_weight, mig)
     mig = mig.astype(jnp.bfloat16)
 
+    half_len = raw.shape[2]
+    early = (half_len // TILE) * TILE - extent + TILE
+    near = early + extent - TILE
+    far = width + extent - TILE - near
+
+    def half(index):
+        return halves[index].reshape(2 * lines, half_len)
+
+    def add_lags(low, high):
+        windows = jnp.concatenate(
+            [full[:, t * TILE + low : t * TILE + high] for t in range(extent // TILE)], axis=0
+        )
+        return dot_nt(windows, chirp_rows[:, low:high])
+
     own.wait()
+
+    @pl.when(rg == 0)
+    def _():
+        full[:, :near] = half(0)[:, :near]
+        sums[...] = add_lags(0, early)
+
+    @pl.when(rg == 1)
+    def _():
+        full[:, far:] = half(1)[:, far - half_len :]
+        sums[...] = add_lags(width - early, width)
+
     pair.wait()
-    half_len = raw.shape[2]
-    full[...] = jnp.concatenate(
-        [halves[0].reshape(2 * lines, half_len), halves[1].reshape(2 * lines, half_len)], axis=1
-    )
-    kernel = chirp_rows[...]
+
+    @pl.when(rg == 0)
+    def _():
+        full[:, near:] = jnp.concatenate([half(0)[:, near:], half(1)], axis=1)
+        sums[...] += add_lags(early, width)
+
+    @pl.when(rg == 1)
+    def _():
+        full[:, :far] = jnp.concatenate([half(0), half(1)[:, : far - half_len]], axis=1)
+        sums[...] += add_lags(0, width - early)
+
+    products = sums[...]
     pieces = []
     for t in range(extent // TILE):
-        product = dot_nt(full[:, t * TILE : t * TILE + width], kernel)
+        product = products[2 * lines * t : 2 * lines * (t + 1)]
         real = product[:lines, :TILE] + product[lines:, TILE:]
         imag = product[lines:, :TILE] - product[:lines, TILE:]
         pieces.append(jnp.concatenate([real, imag], axis=0).astype(jnp.bfloat16))
@@ -282,9 +325,14 @@
     result = pl.pallas_call(
         functools.partial(fused_kernel, azs),
         out_shape=jax.ShapeDtypeStruct((bins, 2, tiles_az, TILE), jnp.float32),
-        in_specs=[pl.BlockSpec(memory_space=pl.ANY), vmem, vmem, vmem, vmem],
+        in_specs=[pl.BlockSpec(memory_space=pltpu.HBM)] * 5,
         out_specs=vmem,
         scratch_shapes=[
+            pltpu.VMEM(chirp.shape, chirp.dtype),
+            pltpu.VMEM(interp_weight.shape, interp_weight.dtype),
+            pltpu.VMEM((1, band_shift.shape[0]), band_shift.dtype),
+            pltpu.VMEM((1, doppler_bin.shape[0]), doppler_bin.dtype),
+            pltpu.SemaphoreType.DMA((4,)),
             pltpu.VMEM((2, 2, lines, half_len), jnp.bfloat16),
             pltpu.VMEM((2 * lines, 2 * half_len), jnp.bfloat16),
             pltpu.VMEM((2 * TILE, taps + TILE), jnp.bfloat16),
@@ -292,6 +340,7 @@
             pltpu.VMEM((slab, 2 * lines), jnp.float32),
             pltpu.VMEM((azs, bins, 2 * lines), jnp.float32),
             pltpu.VMEM((2 * tiles_az, bins, span), jnp.float32),
+            pltpu.VMEM(((2 * half_len - taps) // TILE * 2 * lines, 2 * TILE), jnp.float32),
             pltpu.SemaphoreType.DMA,
             pltpu.SemaphoreType.DMA,
             pltpu.SemaphoreType.DMA,
@@ -299,7 +348,7 @@
             pltpu.SemaphoreType.DMA((azs,)),
         ],
         compiler_params=pltpu.CompilerParams(
-            collective_id=0, has_side_effects=True, vmem_limit_bytes=48 * 1024 * 1024
+            collective_id=0, has_side_effects=True, vmem_limit_bytes=63 * 1024 * 1024
         ),
     )(raw_echo, chirp, interp_weight, band_shift.reshape(1, -1), doppler_bin.reshape(1, -1))
     return result.reshape(bins, 2, tiles_az * TILE)

time: 18.3 us -> 15.4 us (0.84)
  local copies, waits for them, and re-layouts: 3.11 us -> 1.4 us
  Pallas kernels: 14.9 us -> 13.8 us
    unnamed x10 -> x0, local copies, waits for them, and re-layouts: 2.47 us -> none
    pallas_call x1, Pallas kernels: 14.9 us -> 13.8 us  [fused(): pl.pallas_call(functools.partial(fused_kernel, azs), out_shape=jax.ShapeD...]
    reshape x1, local copies, waits for them, and re-layouts: 0.64 us -> 1.4 us  [fused(): return result.reshape(bins, 2, tiles_az * TILE)]
where the time goes in v2:
time: 15.4 us; the launch traced here: 15.2 us
  Pallas kernels  13.8 us (90%)
  local copies, waits for them, and re-layouts  1.4 us (9%)
    pallas_call x1, Pallas kernels, fused(): pl.pallas_call(functools.partial(fused_kernel, azs), out_shape=jax.ShapeD...  13.8 us
    reshape x1, local copies, waits for them, and re-layouts, fused(): return result.reshape(bins, 2, tiles_az * TILE)  1.4 us

profile of v2, /device:TPU:0, one launch (start us, length us, event | category | flops | bytes accessed | tf_op | source)
XLA Modules:
  0.0 15.2 jit_solution(3459382144520863623)
XLA Ops:
  0.0 13.8 %shard_map.55 = f32[8,2,4,128]{3,2,1,0:T(4,128)} custom-call(bf16[2,64,2240]{2,1,0:T(8,128)(2,1)} %raw.1, bf16[2,4096]{1,0:T(2,128)(2,1)} %chirp_in.1, bf16[8,64]{1,0:T(8,128)(2,1)} %weight_in.1, s32[1,64]{1,0:T(1,128)} %bitcast.2, s32[1,128]{1,0:T(1,128)} %bitcast.3), custom_call_target="tpu_custom_call" | custom-call | tf_op jit(solution)/shard_map/pallas_call | solution.py:325
  13.8 1.4 %reshape.11 = f32[8,2,512]{2,1,0:T(2,128)} reshape(f32[8,2,4,128]{3,2,1,0:T(4,128)} %shard_map.55) | data formatting | bytes 65536 | tf_op jit(solution)/shard_map/reshape | solution.py:354

commit v3 on v2

--- a/solution.py
+++ b/solution.py
@@ -204,6 +204,78 @@
             jnp.bfloat16
         )
 
+    position = lax.broadcasted_iota(jnp.int32, (slab, extent), 1)
+    bin_at = lax.broadcasted_iota(jnp.int32, (slab, extent), 0) + rg * slab
+    start = column(shift[...].astype(jnp.float32), 0, slab).astype(jnp.int32)
+    offset = position - bin_at - start
+    mig = jnp.zeros((slab, extent), jnp.float32)
+    for tap in range(weight.shape[0]):
+        tap_weight = column(weight[tap : tap + 1, :].astype(jnp.float32), 0, slab)
+        mig = jnp.where(offset == tap, tap_weight, mig)
+    mig = mig.astype(jnp.bfloat16)
+
+    half_len = raw.shape[2]
+    early = (half_len // TILE) * TILE - extent + TILE
+    near = early + extent - TILE
+    far = width + extent - TILE - near
+
+    def half(index):
+        return halves[index].reshape(2 * lines, half_len)
+
+    def add_lags(low, high):
+        windows = jnp.concatenate(
+            [full[:, t * TILE + low : t * TILE + high] for t in range(extent // TILE)], axis=0
+        )
+        return dot_nt(windows, chirp_rows[:, low:high])
+
+    own.wait()
+
+    @pl.when(rg == 0)
+    def _():
+        full[:, :near] = half(0)[:, :near]
+        sums[...] = add_lags(0, early)
+
+    @pl.when(rg == 1)
+    def _():
+        full[:, far:] = half(1)[:, far - half_len :]
+        sums[...] = add_lags(width - early, width)
+
+    pair.wait()
+
+    @pl.when(rg == 0)
+    def _():
+        full[:, near:] = jnp.concatenate([half(0)[:, near:], half(1)], axis=1)
+        sums[...] += add_lags(early, width)
+
+    @pl.when(rg == 1)
+    def _():
+        full[:, :far] = jnp.concatenate([half(0), half(1)[:, : far - half_len]], axis=1)
+        sums[...] += add_lags(0, width - early)
+
+    products = sums[...]
+    pieces = []
+    for t in range(extent // TILE):
+        product = products[2 * lines * t : 2 * lines * (t + 1)]
+        real = product[:lines, :TILE] + product[lines:, TILE:]
+        imag = product[lines:, :TILE] - product[:lines, TILE:]
+        pieces.append(jnp.concatenate([real, imag], axis=0).astype(jnp.bfloat16))
+    range_lines = jnp.concatenate(pieces, axis=1)
+    moved[...] = dot_nt(mig, range_lines).astype(jnp.bfloat16).astype(jnp.float32)
+
+    def block(index):
+        return moved.at[pl.ds(pl.multiple_of(index * bins, bins), bins), :]
+
+    copies = []
+    for step in range(1, azs):
+        peer = lax.rem(az + step, azs)
+        copy = pltpu.make_async_remote_copy(
+            src_ref=block(peer), dst_ref=slots.at[az], send_sem=turn_send.at[step],
+            recv_sem=turn_recv.at[az], device_id={"az": peer}, device_id_type=MESH,
+        )
+        copy.start()
+        copies.append(copy)
+    slots[az] = block(az)[...]
+
     span = (2 * tiles_az - 1) * TILE
     wheel = span + TILE
     first_bin = rg * slab + az * bins
@@ -219,77 +291,6 @@
             rows = toeplitz_rows(value[b : b + 1, :], TILE)
             az_rows[b, part * TILE : (part + 1) * TILE, :] = rows[:, :span].astype(jnp.bfloat16)
 
-    position = lax.broadcasted_iota(jnp.int32, (slab, extent), 1)
-    bin_at = lax.broadcasted_iota(jnp.int32, (slab, extent), 0) + rg * slab
-    start = column(shift[...].astype(jnp.float32), 0, slab).astype(jnp.int32)
-    offset = position - bin_at - start
-    mig = jnp.zeros((slab, extent), jnp.float32)
-    for tap in range(weight.shape[0]):
-        tap_weight = column(weight[tap : tap + 1, :].astype(jnp.float32), 0, slab)
-        mig = jnp.where(offset == tap, tap_weight, mig)
-    mig = mig.astype(jnp.bfloat16)
-
-    half_len = raw.shape[2]
-    early = (half_len // TILE) * TILE - extent + TILE
-    near = early + extent - TILE
-    far = width + extent - TILE - near
-
-    def half(index):
-        return halves[index].reshape(2 * lines, half_len)
-
-    def add_lags(low, high):
-        windows = jnp.concatenate(
-            [full[:, t * TILE + low : t * TILE + high] for t in range(extent // TILE)], axis=0
-        )
-        return dot_nt(windows, chirp_rows[:, low:high])
-
-    own.wait()
-
-    @pl.when(rg == 0)
-    def _():
-        full[:, :near] = half(0)[:, :near]
-        sums[...] = add_lags(0, early)
-
-    @pl.when(rg == 1)
-    def _():
-        full[:, far:] = half(1)[:, far - half_len :]
-        sums[...] = add_lags(width - early, width)
-
-    pair.wait()
-
-    @pl.when(rg == 0)
-    def _():
-        full[:, near:] = jnp.concatenate([half(0)[:, near:], half(1)], axis=1)
-        sums[...] += add_lags(early, width)
-
-    @pl.when(rg == 1)
-    def _():
-        full[:, :far] = jnp.concatenate([half(0), half(1)[:, : far - half_len]], axis=1)
-        sums[...] += add_lags(0, width - early)
-
-    products = sums[...]
-    pieces = []
-    for t in range(extent // TILE):
-        product = products[2 * lines * t : 2 * lines * (t + 1)]
-        real = product[:lines, :TILE] + product[lines:, TILE:]
-        imag = product[lines:, :TILE] - product[:lines, TILE:]
-        pieces.append(jnp.concatenate([real, imag], axis=0).astype(jnp.bfloat16))
-    range_lines = jnp.concatenate(pieces, axis=1)
-    moved[...] = dot_nt(mig, range_lines).astype(jnp.bfloat16).astype(jnp.float32)
-
-    def block(index):
-        return moved.at[pl.ds(pl.multiple_of(index * bins, bins), bins), :]
-
-    copies = []
-    for step in range(1, azs):
-        peer = lax.rem(az + step, azs)
-        copy = pltpu.make_async_remote_copy(
-            src_ref=block(peer), dst_ref=slots.at[az], send_sem=turn_send.at[step],
-            recv_sem=turn_recv.at[az], device_id={"az": peer}, device_id_type=MESH,
-        )
-        copy.start()
-        copies.append(copy)
-    slots[az] = block(az)[...]
     for step in range(1, azs):
         peer = lax.rem(az + step, azs)
         pltpu.make_async_remote_copy(

time: 15.4 us -> 14.5 us (0.942)
  Pallas kernels: 13.8 us -> 12.9 us
    pallas_call x1, Pallas kernels: 13.8 us -> 12.9 us  [fused(): pl.pallas_call(functools.partial(fused_kernel, azs), out_shape=jax.ShapeD...]
where the time goes in v3:
time: 14.5 us; the launch traced here: 14.4 us
  Pallas kernels  12.9 us (89%)
  local copies, waits for them, and re-layouts  1.4 us (10%)
    pallas_call x1, Pallas kernels, fused(): pl.pallas_call(functools.partial(fused_kernel, azs), out_shape=jax.ShapeD...  12.9 us
    reshape x1, local copies, waits for them, and re-layouts, fused(): return result.reshape(bins, 2, tiles_az * TILE)  1.4 us

profile of v3, /device:TPU:0, one launch (start us, length us, event | category | flops | bytes accessed | tf_op | source)
XLA Modules:
  0.0 14.4 jit_solution(1144868307438638536)
XLA Ops:
  0.0 12.9 %shard_map.55 = f32[8,2,4,128]{3,2,1,0:T(4,128)} custom-call(bf16[2,64,2240]{2,1,0:T(8,128)(2,1)} %raw.1, bf16[2,4096]{1,0:T(2,128)(2,1)} %chirp_in.1, bf16[8,64]{1,0:T(8,128)(2,1)} %weight_in.1, s32[1,64]{1,0:T(1,128)} %bitcast.2, s32[1,128]{1,0:T(1,128)} %bitcast.3), custom_call_target="tpu_custom_call" | custom-call | tf_op jit(solution)/shard_map/pallas_call | solution.py:326
  13.0 1.4 %reshape.11 = f32[8,2,512]{2,1,0:T(2,128)} reshape(f32[8,2,4,128]{3,2,1,0:T(4,128)} %shard_map.55) | data formatting | bytes 65536 | tf_op jit(solution)/shard_map/reshape | solution.py:355

commit v4 on v3

--- a/solution.py
+++ b/solution.py
@@ -277,19 +277,25 @@
     slots[az] = block(az)[...]
 
     span = (2 * tiles_az - 1) * TILE
-    wheel = span + TILE
+    wheel = 2 * TILE
     first_bin = rg * slab + az * bins
-    place = lax.broadcasted_iota(jnp.int32, (bins, wheel), 1)
-    lag = place + AZ_TAPS // 2 - (tiles_az - 1) * TILE - jnp.where(place >= span, wheel, 0)
-    bin_index = first_bin + lax.broadcasted_iota(jnp.int32, (bins, wheel), 0)
+    ring = (2 * tiles_az - 1) * wheel
+    place = lax.broadcasted_iota(jnp.int32, (bins, ring), 1)
+    inner = lax.rem(place, wheel)
+    back = inner - jnp.where(inner < TILE, 0, wheel)
+    lag = place // wheel * TILE + AZ_TAPS // 2 - (tiles_az - 1) * TILE - back
+    bin_index = first_bin + lax.broadcasted_iota(jnp.int32, (bins, ring), 0)
     beta = 0.5 + 0.5 * bin_index.astype(jnp.float32) / (2 * slab)
     rate = column(doppler[...].astype(jnp.float32), first_bin, bins)
     value_re, value_im = filter_taps(lag.astype(jnp.float32), beta, rate)
     for part, value in enumerate((value_re, value_im)):
         value = value.astype(jnp.bfloat16).astype(jnp.float32)
         for b in range(bins):
-            rows = toeplitz_rows(value[b : b + 1, :], TILE)
-            az_rows[b, part * TILE : (part + 1) * TILE, :] = rows[:, :span].astype(jnp.bfloat16)
+            for d in range(2 * tiles_az - 1):
+                rows = toeplitz_rows(value[b : b + 1, d * wheel : (d + 1) * wheel], TILE)
+                az_rows[b, d * TILE : (d + 1) * TILE, part * TILE : (part + 1) * TILE] = rows[
+                    :, :TILE
+                ].astype(jnp.bfloat16)
 
     for step in range(1, azs):
         peer = lax.rem(az + step, azs)
@@ -307,7 +313,9 @@
         for t in range(tiles_az):
             spread[part * tiles_az + t] = signal[:, t * TILE : t * TILE + span]
     for b in range(bins):
-        product = dot_nt(spread[:, b, :].astype(jnp.bfloat16), az_rows[b])
+        product = jnp.dot(
+            spread[:, b, :].astype(jnp.bfloat16), az_rows[b], preferred_element_type=jnp.float32
+        )
         out[b, 0] = product[:tiles_az, :TILE] - product[tiles_az:, TILE:]
         out[b, 1] = product[tiles_az:, :TILE] + product[:tiles_az, TILE:]
     for copy in copies:
@@ -337,7 +345,7 @@
             pltpu.VMEM((2, 2, lines, half_len), jnp.bfloat16),
             pltpu.VMEM((2 * lines, 2 * half_len), jnp.bfloat16),
             pltpu.VMEM((2 * TILE, taps + TILE), jnp.bfloat16),
-            pltpu.VMEM((bins, 2 * TILE, span), jnp.bfloat16),
+            pltpu.VMEM((bins, span, 2 * TILE), jnp.bfloat16),
             pltpu.VMEM((slab, 2 * lines), jnp.float32),
             pltpu.VMEM((azs, bins, 2 * lines), jnp.float32),
             pltpu.VMEM((2 * tiles_az, bins, span), jnp.float32),

time: 14.5 us -> 14.1 us (0.972)
  Pallas kernels: 12.9 us -> 12.5 us
    pallas_call x1, Pallas kernels: 12.9 us -> 12.5 us  [fused(): pl.pallas_call(functools.partial(fused_kernel, azs), out_shape=jax.ShapeD...]
where the time goes in v4:
time: 14.1 us; the launch traced here: 13.9 us
  Pallas kernels  12.5 us (89%)
  local copies, waits for them, and re-layouts  1.4 us (10%)
    pallas_call x1, Pallas kernels, fused(): pl.pallas_call(functools.partial(fused_kernel, azs), out_shape=jax.ShapeD...  12.5 us
    reshape x1, local copies, waits for them, and re-layouts, fused(): return result.reshape(bins, 2, tiles_az * TILE)  1.4 us

profile of v4, /device:TPU:0, one launch (start us, length us, event | category | flops | bytes accessed | tf_op | source)
XLA Modules:
  0.0 13.9 jit_solution(14640494329899340528)
XLA Ops:
  0.0 12.5 %shard_map.55 = f32[8,2,4,128]{3,2,1,0:T(4,128)} custom-call(bf16[2,64,2240]{2,1,0:T(8,128)(2,1)} %raw.1, bf16[2,4096]{1,0:T(2,128)(2,1)} %chirp_in.1, bf16[8,64]{1,0:T(8,128)(2,1)} %weight_in.1, s32[1,64]{1,0:T(1,128)} %bitcast.2, s32[1,128]{1,0:T(1,128)} %bitcast.3), custom_call_target="tpu_custom_call" | custom-call | tf_op jit(solution)/shard_map/pallas_call | solution.py:334
  12.5 1.4 %reshape.11 = f32[8,2,512]{2,1,0:T(2,128)} reshape(f32[8,2,4,128]{3,2,1,0:T(4,128)} %shard_map.55) | data formatting | bytes 65536 | tf_op jit(solution)/shard_map/reshape | solution.py:363

commit v5 on v4

--- a/solution.py
+++ b/solution.py
@@ -204,78 +204,6 @@
             jnp.bfloat16
         )
 
-    position = lax.broadcasted_iota(jnp.int32, (slab, extent), 1)
-    bin_at = lax.broadcasted_iota(jnp.int32, (slab, extent), 0) + rg * slab
-    start = column(shift[...].astype(jnp.float32), 0, slab).astype(jnp.int32)
-    offset = position - bin_at - start
-    mig = jnp.zeros((slab, extent), jnp.float32)
-    for tap in range(weight.shape[0]):
-        tap_weight = column(weight[tap : tap + 1, :].astype(jnp.float32), 0, slab)
-        mig = jnp.where(offset == tap, tap_weight, mig)
-    mig = mig.astype(jnp.bfloat16)
-
-    half_len = raw.shape[2]
-    early = (half_len // TILE) * TILE - extent + TILE
-    near = early + extent - TILE
-    far = width + extent - TILE - near
-
-    def half(index):
-        return halves[index].reshape(2 * lines, half_len)
-
-    def add_lags(low, high):
-        windows = jnp.concatenate(
-            [full[:, t * TILE + low : t * TILE + high] for t in range(extent // TILE)], axis=0
-        )
-        return dot_nt(windows, chirp_rows[:, low:high])
-
-    own.wait()
-
-    @pl.when(rg == 0)
-    def _():
-        full[:, :near] = half(0)[:, :near]
-        sums[...] = add_lags(0, early)
-
-    @pl.when(rg == 1)
-    def _():
-        full[:, far:] = half(1)[:, far - half_len :]
-        sums[...] = add_lags(width - early, width)
-
-    pair.wait()
-
-    @pl.when(rg == 0)
-    def _():
-        full[:, near:] = jnp.concatenate([half(0)[:, near:], half(1)], axis=1)
-        sums[...] += add_lags(early, width)
-
-    @pl.when(rg == 1)
-    def _():
-        full[:, :far] = jnp.concatenate([half(0), half(1)[:, : far - half_len]], axis=1)
-        sums[...] += add_lags(0, width - early)
-
-    products = sums[...]
-    pieces = []
-    for t in range(extent // TILE):
-        product = products[2 * lines * t : 2 * lines * (t + 1)]
-        real = product[:lines, :TILE] + product[lines:, TILE:]
-        imag = product[lines:, :TILE] - product[:lines, TILE:]
-        pieces.append(jnp.concatenate([real, imag], axis=0).astype(jnp.bfloat16))
-    range_lines = jnp.concatenate(pieces, axis=1)
-    moved[...] = dot_nt(mig, range_lines).astype(jnp.bfloat16).astype(jnp.float32)
-
-    def block(index):
-        return moved.at[pl.ds(pl.multiple_of(index * bins, bins), bins), :]
-
-    copies = []
-    for step in range(1, azs):
-        peer = lax.rem(az + step, azs)
-        copy = pltpu.make_async_remote_copy(
-            src_ref=block(peer), dst_ref=slots.at[az], send_sem=turn_send.at[step],
-            recv_sem=turn_recv.at[az], device_id={"az": peer}, device_id_type=MESH,
-        )
-        copy.start()
-        copies.append(copy)
-    slots[az] = block(az)[...]
-
     span = (2 * tiles_az - 1) * TILE
     wheel = 2 * TILE
     first_bin = rg * slab + az * bins
@@ -288,6 +216,79 @@
     beta = 0.5 + 0.5 * bin_index.astype(jnp.float32) / (2 * slab)
     rate = column(doppler[...].astype(jnp.float32), first_bin, bins)
     value_re, value_im = filter_taps(lag.astype(jnp.float32), beta, rate)
+
+    position = lax.broadcasted_iota(jnp.int32, (slab, extent), 1)
+    bin_at = lax.broadcasted_iota(jnp.int32, (slab, extent), 0) + rg * slab
+    start = column(shift[...].astype(jnp.float32), 0, slab).astype(jnp.int32)
+    offset = position - bin_at - start
+    mig = jnp.zeros((slab, extent), jnp.float32)
+    for tap in range(weight.shape[0]):
+        tap_weight = column(weight[tap : tap + 1, :].astype(jnp.float32), 0, slab)
+        mig = jnp.where(offset == tap, tap_weight, mig)
+    mig = mig.astype(jnp.bfloat16)
+
+    half_len = raw.shape[2]
+    early = (half_len // TILE) * TILE - extent + TILE
+    near = early + extent - TILE
+    far = width + extent - TILE - near
+
+    def half(index):
+        return halves[index].reshape(2 * lines, half_len)
+
+    def add_lags(low, high):
+        windows = jnp.concatenate(
+            [full[:, t * TILE + low : t * TILE + high] for t in range(extent // TILE)], axis=0
+        )
+        return dot_nt(windows, chirp_rows[:, low:high])
+
+    own.wait()
+
+    @pl.when(rg == 0)
+    def _():
+        full[:, :near] = half(0)[:, :near]
+        sums[...] = add_lags(0, early)
+
+    @pl.when(rg == 1)
+    def _():
+        full[:, far:] = half(1)[:, far - half_len :]
+        sums[...] = add_lags(width - early, width)
+
+    pair.wait()
+
+    @pl.when(rg == 0)
+    def _():
+        full[:, near:] = jnp.concatenate([half(0)[:, near:], half(1)], axis=1)
+        sums[...] += add_lags(early, width)
+
+    @pl.when(rg == 1)
+    def _():
+        full[:, :far] = jnp.concatenate([half(0), half(1)[:, : far - half_len]], axis=1)
+        sums[...] += add_lags(0, width - early)
+
+    products = sums[...]
+    pieces = []
+    for t in range(extent // TILE):
+        product = products[2 * lines * t : 2 * lines * (t + 1)]
+        real = product[:lines, :TILE] + product[lines:, TILE:]
+        imag = product[lines:, :TILE] - product[:lines, TILE:]
+        pieces.append(jnp.concatenate([real, imag], axis=0).astype(jnp.bfloat16))
+    range_lines = jnp.concatenate(pieces, axis=1)
+    moved[...] = dot_nt(mig, range_lines).astype(jnp.bfloat16).astype(jnp.float32)
+
+    def block(index):
+        return moved.at[pl.ds(pl.multiple_of(index * bins, bins), bins), :]
+
+    copies = []
+    for step in range(1, azs):
+        peer = lax.rem(az + step, azs)
+        copy = pltpu.make_async_remote_copy(
+            src_ref=block(peer), dst_ref=slots.at[az], send_sem=turn_send.at[step],
+            recv_sem=turn_recv.at[az], device_id={"az": peer}, device_id_type=MESH,
+        )
+        copy.start()
+        copies.append(copy)
+    slots[az] = block(az)[...]
+
     for part, value in enumerate((value_re, value_im)):
         value = value.astype(jnp.bfloat16).astype(jnp.float32)
         for b in range(bins):

time: 14.1 us -> 14.1 us (level)
  no operation moved by 1% of the time
where the time goes in v5:
time: 14.1 us; the launch traced here: 13.9 us
  Pallas kernels  12.5 us (89%)
  local copies, waits for them, and re-layouts  1.4 us (10%)
    pallas_call x1, Pallas kernels, fused(): pl.pallas_call(functools.partial(fused_kernel, azs), out_shape=jax.ShapeD...  12.5 us
    reshape x1, local copies, waits for them, and re-layouts, fused(): return result.reshape(bins, 2, tiles_az * TILE)  1.4 us

profile of v5, /device:TPU:0, one launch (start us, length us, event | category | flops | bytes accessed | tf_op | source)
XLA Modules:
  0.0 13.9 jit_solution(14505324021102852860)
XLA Ops:
  0.0 12.5 %shard_map.55 = f32[8,2,4,128]{3,2,1,0:T(4,128)} custom-call(bf16[2,64,2240]{2,1,0:T(8,128)(2,1)} %raw.1, bf16[2,4096]{1,0:T(2,128)(2,1)} %chirp_in.1, bf16[8,64]{1,0:T(8,128)(2,1)} %weight_in.1, s32[1,64]{1,0:T(1,128)} %bitcast.2, s32[1,128]{1,0:T(1,128)} %bitcast.3), custom_call_target="tpu_custom_call" | custom-call | tf_op jit(solution)/shard_map/pallas_call | solution.py:335
  12.5 1.4 %reshape.11 = f32[8,2,512]{2,1,0:T(2,128)} reshape(f32[8,2,4,128]{3,2,1,0:T(4,128)} %shard_map.55) | data formatting | bytes 65536 | tf_op jit(solution)/shard_map/reshape | solution.py:364
